TPU v7x, 512 devices: a whole 4x8x8 slice. The times are simulated.
512 devices in a mesh: section: 32 (over z, x_hi, core), tensor: 16 (over x_lo, y).
Axes of the slice: x: 4 (x_hi: 2, x_lo: 2; x = x_hi * 2 + x_lo), y: 8, z: 8, core: 2. Of those that a mesh axis runs over, the one named last changes fastest.
Arguments:
- held: bfloat16 [32, 2, 256, 12288], P('section', None, None, 'tensor'), may hold values from -6 to 6
- norm_gain: float32 [32, 2, 12288], P('section', None, 'tensor'), may hold values from 0.1 to 1.9
- key_gain: float32 [32, 2, 12288], P('section', None, 'tensor'), may hold values from -2 to 2
- evict_slot: int32 [32], P('section'), may hold values from 0 to 1
- evict_step: int32 [32], P('section'), may hold values from 0 to 1
Outputs:
- final: bfloat16 [32, 2, 256, 12288], P('section', None, None, 'tensor')
- mirror_store: bfloat16 [32, 256, 12288], P('section', None, 'tensor')
All inputs are finite; a program needn't handle non-finite values.
Results may differ from a plain program's by a relative error of at most 0.039.
Values may be sent and summed in bfloat16 or wider, within the bound.
No kernel may reach another device: no remote copies, remote signals or barrier semaphores. Data moves between devices by JAX's collectives and lax.ppermute only.
A program may use at most 64 MiB of HBM per device.

v0:
```python
import functools

import jax
import jax.numpy as jnp
from jax import lax
from jax.experimental import pallas as pl
from jax.experimental.pallas import tpu as pltpu
from jax.sharding import PartitionSpec as P

D = 12288
HEAD = 128
LAYERS = 2
BLOCK = 128
EPS = 1e-5
SCORE = 1.4426950408889634 / HEAD**0.5
X_LO = X_HI = CORES = 2

VMEM = pl.BlockSpec(memory_space=pltpu.VMEM)
PARAMS = pltpu.CompilerParams(vmem_limit_bytes=32 * 1024 * 1024)


def call(kernel, out_shape, name, mflop=1, scratch=()):
    several = isinstance(out_shape, tuple)

    def run(*operands):
        return pl.pallas_call(
            kernel,
            out_shape=out_shape,
            in_specs=[VMEM] * len(operands),
            out_specs=(VMEM,) * len(out_shape) if several else VMEM,
            scratch_shapes=[pltpu.VMEM(like.shape, like.dtype) for like in scratch],
            compiler_params=PARAMS,
            cost_estimate=pl.CostEstimate(
                flops=mflop * 1_000_000, bytes_accessed=1_000_000, transcendentals=mflop * 2_000
            ),
            name=name,
        )(*operands)

    return run


def f32(*shape):
    return jax.ShapeDtypeStruct(shape, jnp.float32)


def bf16(*shape):
    return jax.ShapeDtypeStruct(shape, jnp.bfloat16)


def column(total):
    inv = lax.rsqrt(total / D + EPS)
    rows = [jnp.broadcast_to(inv[i : i + 1], (BLOCK, BLOCK)).T for i in range(inv.shape[0])]
    return jnp.concatenate(rows, axis=0)


def head_layer(xf, scale, ngain, kgain):
    length = xf.shape[0]
    keep = lax.broadcasted_iota(jnp.int32, (BLOCK, BLOCK), 1) <= lax.broadcasted_iota(jnp.int32, (BLOCK, BLOCK), 0)
    h = xf * scale * ngain
    query = h.astype(jnp.bfloat16)
    keys = (h * (kgain * SCORE)).astype(jnp.bfloat16)
    values = jnp.concatenate([query, jnp.ones((length, HEAD), jnp.bfloat16)], axis=1)
    out = []
    for i in range(length // BLOCK):
        here = slice(i * BLOCK, (i + 1) * BLOCK)
        seen = (i + 1) * BLOCK
        s = lax.dot_general(
            query[here], keys[:seen], (((1,), (1,)), ((), ())), preferred_element_type=jnp.float32
        )
        last = jnp.where(keep, s[:, i * BLOCK :], jnp.float32(-1e30))
        s = last if i == 0 else jnp.concatenate([s[:, : i * BLOCK], last], axis=1)
        p = jnp.exp2(s - jnp.max(s, axis=1, keepdims=True)).astype(jnp.bfloat16)
        o = jnp.dot(p, values[:seen], preferred_element_type=jnp.float32)
        out.append((xf[here] + o[:, :HEAD] / o[:, HEAD:]).astype(jnp.bfloat16))
    return jnp.concatenate(out, axis=0)


def token_sums(squares, out_ref):
    rows = []
    for sq in squares:
        for i in range(sq.shape[0] // BLOCK):
            rows.append(jnp.sum(sq[i * BLOCK : (i + 1) * BLOCK].T, axis=0, keepdims=True))
    out_ref[...] = jnp.broadcast_to(jnp.concatenate(rows, axis=0)[None], out_ref.shape)


def lanes(head):
    return slice(head * HEAD, (head + 1) * HEAD)


class Pack:
    def __init__(self, heads, batch, blocks):
        self.heads, self.rows = heads, batch * blocks
        self.slot = 2 * LAYERS * heads
        self.step = self.slot + 1
        self.size = -(-(self.step + 1) // 8) * 8
        self.full = 2 * self.size + 2 * LAYERS * self.rows

    def gains(self, ref, layer, head):
        base = layer // LAYERS * self.size
        at = [base + (part * LAYERS + layer % LAYERS) * self.heads + head for part in range(2)]
        return [ref[i : i + 1, :] for i in at]

    def sums(self, layer):
        return slice(2 * self.size + layer * self.rows, 2 * self.size + (layer + 1) * self.rows)

    def second(self, ref, section=0):
        at = section * self.size + self.slot
        return ref[at : at + 1, :] > 0.5

    def late(self, ref, section=0):
        at = section * self.size + self.step
        return ref[at : at + 1, :] > 0.5


def first_kernel(x_ref, out_ref):
    batch, _, width = x_ref.shape
    found = []
    for b in range(batch):
        sq = 0.0
        for head in range(width // HEAD):
            xf = x_ref[b, :, lanes(head)].astype(jnp.float32)
            sq = sq + xf * xf
        found.append(sq)
    token_sums(found, out_ref)


def one_layer(pack, layer, x_refs, totals, pack_ref, y_ref):
    blocks = x_refs[0].shape[0] // BLOCK
    found = []
    for b, x_ref in enumerate(x_refs):
        scale = column(totals[b * blocks : (b + 1) * blocks])
        sq = 0.0
        for head in range(pack.heads):
            xf = x_ref[:, lanes(head)].astype(jnp.float32)
            y = head_layer(xf, scale, *pack.gains(pack_ref, layer, head))
            if y_ref is not None:
                y_ref[b, :, lanes(head)] = y
            yf = y.astype(jnp.float32)
            sq = sq + yf * yf
        found.append(sq)
    return found


def layer_kernel(pack, layer, outputs, x_ref, parts_ref, pack_ref, *refs):
    refs = list(refs)
    next_ref = refs.pop(0) if "pick" in outputs else None
    y_ref = refs.pop(0) if "y" in outputs else None
    pick_ref = refs.pop(0) if "pick" in outputs else None
    x_refs = [x_ref.at[b] for b in range(x_ref.shape[0])]
    found = one_layer(pack, layer, x_refs, jnp.sum(parts_ref[...], axis=0), pack_ref, y_ref)
    if pick_ref is not None:
        second = pack.second(next_ref)
        for head in range(pack.heads):
            pick_ref[:, lanes(head)] = either(second, y_ref[1, :, lanes(head)], y_ref[0, :, lanes(head)])
    token_sums(found, refs[-1])


def either(condition, there, here):
    return jnp.where(condition, there.astype(jnp.float32), here.astype(jnp.float32)).astype(jnp.bfloat16)


def choose_kernel(pack, y_ref, carry_ref, pack_ref, out_ref):
    second, late = pack.second(pack_ref), pack.late(pack_ref)
    for head in range(pack.heads):
        at = lanes(head)
        out_ref[:, at] = either(late, carry_ref[:, at], either(second, y_ref[1, :, at], y_ref[0, :, at]))


def pack_kernel(pack, own_ref, next_ref, *refs):
    *parts_refs, out_ref = refs
    out_ref[: pack.size, :] = own_ref[...]
    out_ref[pack.size : 2 * pack.size, :] = next_ref[...]
    for layer, parts_ref in enumerate(parts_refs):
        out_ref[pack.sums(layer), :] = jnp.sum(parts_ref[...], axis=0)


def repeat_kernel(pack, x0_ref, x1_ref, pack_ref, out_ref, a_ref, b_ref):
    refs = [(x0_ref, x1_ref), a_ref, b_ref, a_ref, out_ref]
    for layer in range(2 * LAYERS):
        x_refs = [refs[layer].at[b] for b in range(out_ref.shape[0])] if layer else refs[0]
        one_layer(pack, layer, x_refs, pack_ref[pack.sums(layer), :], pack_ref, refs[layer + 1])


def mirror_kernel(pack, x_ref, pack_ref, out_ref, y_ref):
    blocks = x_ref.shape[0] // BLOCK
    second, late = pack.second(pack_ref, 1), pack.late(pack_ref, 1)
    refs = [x_ref, y_ref, out_ref]
    for at in range(LAYERS):
        layer = LAYERS + at
        totals = pack_ref[pack.sums(layer), :]
        scale = column(jnp.where(second, totals[blocks : 2 * blocks], totals[:blocks]))
        for head in range(pack.heads):
            xf = refs[at][:, lanes(head)].astype(jnp.float32)
            y = head_layer(xf, scale, *pack.gains(pack_ref, layer, head))
            if at == LAYERS - 1:
                y = either(late, y, x_ref[:, lanes(head)])
            refs[at + 1][:, lanes(head)] = y


def exchange(parts):
    return lax.all_to_all(parts, "tensor", 0, 0, tiled=True)


def send(value, target):
    count = lax.axis_size("section")
    return lax.ppermute(value, "section", [(s, target(s) % count) for s in range(count)])


def around_x(hop):
    sections, members = lax.axis_size("section"), lax.axis_size("tensor")
    ys, count = members // X_LO, X_HI * X_LO
    layers_z = sections // (X_HI * CORES)

    def flat(z, x, core, y):
        x %= count
        return (((z % layers_z) * X_HI + x // X_LO) * CORES + core) * members + (x % X_LO) * ys + y

    pairs = []
    for z in range(layers_z):
        for x in range(count):
            for core in range(CORES):
                for y in range(ys):
                    middle = flat(z, x + 1, core, y)
                    pairs.append(
                        (middle, flat(z + x // X_LO, x + 2, core, y)) if hop else (flat(z, x, core, y), middle)
                    )
    return pairs


def after(value, *earlier):
    return lax.optimization_barrier((value, *earlier))[0]


def shards(held, norm_gain, key_gain, evict_slot, evict_step):
    x = held[0]
    batch, length, width = x.shape
    heads = width // HEAD
    pack = Pack(heads, batch, length // BLOCK)
    sections, members = lax.axis_size("section"), lax.axis_size("tensor")
    both, one = bf16(*x.shape), bf16(length, width)
    sums = f32(members, pack.rows, BLOCK)
    axes = ("section", "tensor")

    def layer(at, *outputs):
        shapes = {"y": both, "pick": one, "sums": sums}
        return call(functools.partial(layer_kernel, pack, at, outputs), tuple(shapes[name] for name in outputs), "layer", 400)

    facts = jnp.concatenate([evict_slot, evict_step]).astype(jnp.float32)
    own = jnp.concatenate(
        [
            norm_gain.reshape(-1, HEAD),
            key_gain.reshape(-1, HEAD),
            jnp.broadcast_to(facts[:, None], (2, HEAD)),
            jnp.zeros((pack.size - pack.step - 1, HEAD), jnp.float32),
        ],
        axis=0,
    )

    halfway = lax.ppermute(x[1], axes, around_x(0))
    found = call(first_kernel, sums, "first_sums")(x)
    moved0 = send(after(x[0], found), lambda s: s + 2)
    parts = [exchange(found)]
    y, found = layer(0, "y", "sums")(x, parts[0], own)
    moved1 = lax.ppermute(after(halfway, found), axes, around_x(1))
    ahead = send(after(own, found), lambda s: s - 1)
    parts.append(exchange(found))
    y, pick, found = layer(1, "y", "pick", "sums")(y, parts[1], own, ahead)
    carry = send(after(pick, found), lambda s: s + 1)
    parts.append(exchange(found))
    (found,) = layer(0, "sums")(y, parts[2], ahead)
    chosen = call(functools.partial(choose_kernel, pack), one, "choose")(y, after(carry, found), own)
    kept = send(chosen, lambda s: sections - 1 - s)
    parts.append(exchange(found))
    full = call(functools.partial(pack_kernel, pack), f32(pack.full, HEAD), "pack")(own, ahead, *parts)
    behind = send(full, lambda s: s + 2)
    mirrored = send(full, lambda s: sections - 2 - s)

    repeat = functools.partial(repeat_kernel, pack)
    final = call(repeat, both, "repeat", 1600, [both, both])(moved0, moved1, behind)
    stored = call(functools.partial(mirror_kernel, pack), one, "mirror", 400, [one])(kept, mirrored)
    return (final[None], stored[None])


def solution(mesh):
    return jax.shard_map(
        shards,
        mesh=mesh,
        in_specs=(
            P("section", None, None, "tensor"),
            P("section", None, "tensor"),
            P("section", None, "tensor"),
            P("section"),
            P("section"),
        ),
        out_specs=(P("section", None, None, "tensor"), P("section", None, "tensor")),
        check_vma=False,
    )
```

profile of v0, /device:TPU:8, one launch (start us, length us, event | category | flops | bytes accessed | tf_op | source)
XLA Modules:
  0.0 106.1 jit_solution(12028412980637074101)
XLA Ops:
  0.6 0.0 copy-start
  0.6 1.1 %copy-done = bf16[1,2,256,768]{3,2,1,0:T(8,128)(2,1)S(1)} copy-done((bf16[1,2,256,768]{3,2,1,0:T(8,128)(2,1)S(1)}, bf16[1,2,256,768]{3,2,1,0:T(8,128)(2,1)}, u32[]{:S(2)}) %copy-start) | copy-done | bytes 786456
  1.8 0.0 copy-start.1
  1.8 0.8 first_sums.1
  2.6 9.1 %all-to-all-start = ((f32[16,4,128]{2,1,0:T(4,128)}), f32[16,4,128]{2,1,0:T(4,128)S(1)}, u32[]{:S(2)}, u32[]{:S(2)}) async-start(f32[16,4,128]{2,1,0:T(4,128)} %first_sums.1), calls=%async_computation | async-start | bytes 65536 | tf_op jit(solution)/shard_map/all_to_all | solution.py:201
  11.7 0.0 copy-done.1
  11.7 0.0 copy-start.2
  11.7 0.1 slice_bitcast_fusion
  11.8 0.0 copy-start.3
  11.8 3.4 %collective-permute-start.1 = (bf16[256,768]{1,0:T(8,128)(2,1)S(1)}, bf16[256,768]{1,0:T(8,128)(2,1)S(1)}, u32[]{:S(2)}, u32[]{:S(2)}) collective-permute-start(bf16[256,768]{1,0:T(8,128)(2,1)S(1)} %get-tuple-element.22), channel_id=1, source_target_pairs={{0,8},{1,9},{2,10},{3,11},{4,12},{5,13},{6,14},{7,15},{16,24},{17,... | collective-permute-start | bytes 1179656 | tf_op jit(solution)/shard_map/ppermute | solution.py:259
  15.2 0.0 copy-done.2
  15.3 0.0 copy-done.3
  16.6 0.1 add_convert_fusion
  16.7 0.1 pad.2.clone
  16.7 0.1 pad.3.clone
  16.8 0.1 maximum_maximum_fusion.pack_ref.own_ref
  16.9 2.1 %all-to-all-done.parts_ref.refs_0_ = f32[16,4,128]{2,1,0:T(4,128)S(1)} async-done(((f32[16,4,128]{2,1,0:T(4,128)}), f32[16,4,128]{2,1,0:T(4,128)S(1)}, u32[]{:S(2)}, u32[]{:S(2)}) %all-to-all-start) | async-done | bytes 32800 | tf_op jit(solution)/shard_map/all_to_all | solution.py:201
  19.0 2.4 %layer.3 = (bf16[2,256,768]{2,1,0:T(8,128)(2,1)S(1)}, f32[16,4,128]{2,1,0:T(4,128)}) custom-call(bf16[2,256,768]{2,1,0:T(8,128)(2,1)S(1)} %bitcast.8, f32[16,4,128]{2,1,0:T(4,128)S(1)} %all-to-all-done.parts_ref.refs_0_, f32[32,128]{1,0:T(8,128)S(1)} %maximum_maximum_fusion.pack_ref.own_ref), custom_call_target="tpu_custom_call" | custom-call | flops 400000000 | bytes 1000000 | tf_op jit(solution)/shard_map/layer/pallas_call | solution.py:26
  21.4 5.1 %all-to-all-start.1 = ((f32[16,4,128]{2,1,0:T(4,128)}), f32[16,4,128]{2,1,0:T(4,128)S(1)}, u32[]{:S(2)}, u32[]{:S(2)}) async-start(f32[16,4,128]{2,1,0:T(4,128)} %get-tuple-element.13), calls=%async_computation.1 | async-start | bytes 65536 | tf_op jit(solution)/shard_map/all_to_all | solution.py:201
  26.6 10.5 %collective-permute-start.3 = (f32[32,128]{1,0:T(8,128)S(1)}, f32[32,128]{1,0:T(8,128)S(1)}, u32[]{:S(2)}, u32[]{:S(2)}) collective-permute-start(f32[32,128]{1,0:T(8,128)S(1)} %maximum_maximum_fusion.pack_ref.own_ref), channel_id=1, source_target_pairs={{0,496},{16,0},{32,16},{48,32},{64,48},{80,64},{96,80},{112,96},{1... | collective-permute-start | bytes 49160 | tf_op jit(solution)/shard_map/ppermute | solution.py:206
  37.0 1.4 %collective-permute-done.3.refs_0_.pack_ref.next_ref = f32[32,128]{1,0:T(8,128)S(1)} collective-permute-done((f32[32,128]{1,0:T(8,128)S(1)}, f32[32,128]{1,0:T(8,128)S(1)}, u32[]{:S(2)}, u32[]{:S(2)}) %collective-permute-start.3) | collective-permute-done | bytes 16416 | tf_op jit(solution)/shard_map/ppermute | solution.py:206
  38.4 0.0 all-to-all-done.1.parts_ref.refs_1_
  38.4 2.0 %layer.4 = (bf16[2,256,768]{2,1,0:T(8,128)(2,1)S(1)}, bf16[256,768]{1,0:T(8,128)(2,1)S(1)}, f32[16,4,128]{2,1,0:T(4,128)S(1)}) custom-call(bf16[2,256,768]{2,1,0:T(8,128)(2,1)S(1)} %get-tuple-element.16.x_ref, f32[16,4,128]{2,1,0:T(4,128)S(1)} %all-to-all-done.1.parts_ref.refs_1_, f32[32,128]{1,0:T(8,128)S(1)} %maximum_maximum_fusion.pack_ref.own_ref, ...), custom_call_target="tpu_custom_call" | custom-call | flops 400000000 | bytes 1000000 | tf_op jit(solution)/shard_map/layer/pallas_call | solution.py:26
  40.4 1.9 %collective-permute-start.5 = (bf16[256,768]{1,0:T(8,128)(2,1)S(1)}, bf16[256,768]{1,0:T(8,128)(2,1)S(1)}, u32[]{:S(2)}, u32[]{:S(2)}) collective-permute-start(bf16[256,768]{1,0:T(8,128)(2,1)S(1)} %get-tuple-element.20), channel_id=1, source_target_pairs={{0,16},{16,32},{32,48},{48,64},{64,80},{80,96},{96,112},{112,128},... | collective-permute-start | bytes 1179656 | tf_op jit(solution)/shard_map/ppermute | solution.py:206
  42.4 1.9 %collective-permute-start = (bf16[256,768]{1,0:T(8,128)(2,1)S(1)}, bf16[256,768]{1,0:T(8,128)(2,1)S(1)}, u32[]{:S(2)}, u32[]{:S(2)}) collective-permute-start(bf16[256,768]{1,0:T(8,128)(2,1)S(1)} %get-tuple-element.12), channel_id=1, source_target_pairs={{0,32},{16,48},{32,64},{48,80},{64,96},{80,112},{96,128},{112,144}... | collective-permute-start | bytes 1179656 | tf_op jit(solution)/shard_map/ppermute | solution.py:206
  44.3 0.0 collective-permute-done.1
  44.3 2.0 %collective-permute-start.2 = (bf16[256,768]{1,0:T(8,128)(2,1)S(1)}, bf16[256,768]{1,0:T(8,128)(2,1)S(1)}, u32[]{:S(2)}, u32[]{:S(2)}) collective-permute-start(bf16[256,768]{1,0:T(8,128)(2,1)S(1)} %collective-permute-done.1), channel_id=1, source_target_pairs={{8,32},{9,33},{10,34},{11,35},{12,36},{13,37},{14,38},{15,39},{24,... | collective-permute-start | bytes 1179656 | tf_op jit(solution)/shard_map/ppermute | solution.py:264
  46.3 16.1 %all_to_all.20.parts_ref.refs_2_ = f32[16,4,128]{2,1,0:T(4,128)S(1)} all-to-all(f32[16,4,128]{2,1,0:T(4,128)S(1)} %get-tuple-element.17), channel_id=1, replica_groups=mesh['section'=32,'tensor'=16] {'tensor'}, dimensions={0} | all-to-all | bytes 65536 | tf_op jit(solution)/shard_map/all_to_all | solution.py:201
  62.4 1.8 %layer.5 = f32[16,4,128]{2,1,0:T(4,128)S(1)} custom-call(bf16[2,256,768]{2,1,0:T(8,128)(2,1)S(1)} %get-tuple-element.18.x_ref.y_ref, f32[16,4,128]{2,1,0:T(4,128)S(1)} %all_to_all.20.parts_ref.refs_2_, f32[32,128]{1,0:T(8,128)S(1)} %collective-permute-done.3.refs_0_.pack_ref.next_ref), custom_call_target="tpu_custom_call" | custom-call | flops 400000000 | bytes 1000000 | tf_op jit(solution)/shard_map/layer/pallas_call | solution.py:26
  64.2 0.0 collective-permute-done.5.carry_ref
  64.2 0.2 choose.1
  64.3 11.6 %collective-permute-start.6 = (bf16[256,768]{1,0:T(8,128)(2,1)S(1)}, bf16[256,768]{1,0:T(8,128)(2,1)S(1)}, u32[]{:S(2)}, u32[]{:S(2)}) collective-permute-start(bf16[256,768]{1,0:T(8,128)(2,1)S(1)} %choose.1), channel_id=1, source_target_pairs={{0,496},{16,480},{32,464},{48,448},{64,432},{80,416},{96,400},{112... | collective-permute-start | bytes 1179656 | tf_op jit(solution)/shard_map/ppermute | solution.py:206
  76.0 12.2 %all_to_all.21.refs_3_ = f32[16,4,128]{2,1,0:T(4,128)S(1)} all-to-all(f32[16,4,128]{2,1,0:T(4,128)S(1)} %layer.5), channel_id=1, replica_groups=mesh['section'=32,'tensor'=16] {'tensor'}, dimensions={0} | all-to-all | bytes 65536 | tf_op jit(solution)/shard_map/all_to_all | solution.py:201
  88.2 4.0 %collective-permute-start.4 = (f32[80,128]{1,0:T(8,128)S(1)}, f32[80,128]{1,0:T(8,128)S(1)}, u32[]{:S(2)}, u32[]{:S(2)}) collective-permute-start(f32[80,128]{1,0:T(8,128)S(1)} %pack.1), channel_id=1, source_target_pairs={{0,32},{16,48},{32,64},{48,80},{64,96},{80,112},{96,128},{112,144}... | collective-permute-start | bytes 122888 | tf_op jit(solution)/shard_map/ppermute | solution.py:206
  92.2 5.6 %collective-permute-start.7 = (f32[80,128]{1,0:T(8,128)S(1)}, f32[80,128]{1,0:T(8,128)S(1)}, u32[]{:S(2)}, u32[]{:S(2)}) collective-permute-start(f32[80,128]{1,0:T(8,128)S(1)} %pack.1), channel_id=1, source_target_pairs={{0,480},{16,464},{32,448},{48,432},{64,416},{80,400},{96,384},{112... | collective-permute-start | bytes 122888 | tf_op jit(solution)/shard_map/ppermute | solution.py:206
  97.9 0.0 collective-permute-done.4.pack_ref
  97.9 0.0 collective-permute-done.x0_ref
  97.9 0.0 collective-permute-done.2.x1_ref
  97.9 5.7 %repeat.1 = bf16[2,256,768]{2,1,0:T(8,128)(2,1)} custom-call(bf16[256,768]{1,0:T(8,128)(2,1)S(1)} %collective-permute-done.x0_ref, bf16[256,768]{1,0:T(8,128)(2,1)S(1)} %collective-permute-done.2.x1_ref, f32[80,128]{1,0:T(8,128)S(1)} %collective-permute-done.4.pack_ref), custom_call_target="tpu_custom_call" | custom-call | flops 1600000000 | bytes 1000000 | tf_op jit(solution)/shard_map/repeat/pallas_call | solution.py:26
  103.6 0.0 collective-permute-done.7.pack_ref
  103.6 0.0 collective-permute-done.6.x_ref
  103.6 2.4 %mirror.1 = bf16[256,768]{1,0:T(8,128)(2,1)} custom-call(bf16[256,768]{1,0:T(8,128)(2,1)S(1)} %collective-permute-done.6.x_ref, f32[80,128]{1,0:T(8,128)S(1)} %collective-permute-done.7.pack_ref), custom_call_target="tpu_custom_call" | custom-call | flops 400000000 | bytes 1000000 | tf_op jit(solution)/shard_map/mirror/pallas_call | solution.py:26
  (4 shorter events, 0.1 us)
Async XLA Ops:
  0.6 1.1 %copy-start = (bf16[1,2,256,768]{3,2,1,0:T(8,128)(2,1)S(1)}, bf16[1,2,256,768]{3,2,1,0:T(8,128)(2,1)}, u32[]{:S(2)}) copy-start(bf16[1,2,256,768]{3,2,1,0:T(8,128)(2,1)} %param.5) | copy-start | bytes 2359300
  1.8 10.0 %copy-start.1 = (bf16[1,2,256,768]{3,2,1,0:T(8,128)(2,1)S(1)}, bf16[1,2,256,768]{3,2,1,0:T(8,128)(2,1)}, u32[]{:S(2)}) copy-start(bf16[1,2,256,768]{3,2,1,0:T(8,128)(2,1)} %param.5) | copy-start | bytes 2359300
  2.6 16.4 %all-to-all-start = ((f32[16,4,128]{2,1,0:T(4,128)}), f32[16,4,128]{2,1,0:T(4,128)S(1)}, u32[]{:S(2)}, u32[]{:S(2)}) async-start(f32[16,4,128]{2,1,0:T(4,128)} %first_sums.1), calls=%async_computation | async-start | bytes 65536 | tf_op jit(solution)/shard_map/all_to_all | solution.py:201
  11.7 3.5 %copy-start.2 = (f32[1,2,768]{2,1,0:T(2,128)S(1)}, f32[1,2,768]{2,1,0:T(2,128)}, u32[]{:S(2)}) copy-start(f32[1,2,768]{2,1,0:T(2,128)} %param.6) | copy-start | bytes 18436
  11.8 3.5 %copy-start.3 = (f32[1,2,768]{2,1,0:T(2,128)S(1)}, f32[1,2,768]{2,1,0:T(2,128)}, u32[]{:S(2)}) copy-start(f32[1,2,768]{2,1,0:T(2,128)} %param.7) | copy-start | bytes 18436
  11.8 32.5 %collective-permute-start.1 = (bf16[256,768]{1,0:T(8,128)(2,1)S(1)}, bf16[256,768]{1,0:T(8,128)(2,1)S(1)}, u32[]{:S(2)}, u32[]{:S(2)}) collective-permute-start(bf16[256,768]{1,0:T(8,128)(2,1)S(1)} %get-tuple-element.22), channel_id=1, source_target_pairs={{0,8},{1,9},{2,10},{3,11},{4,12},{5,13},{6,14},{7,15},{16,24},{17,... | collective-permute-start | bytes 1179656 | tf_op jit(solution)/shard_map/ppermute | solution.py:259
  21.4 17.0 %all-to-all-start.1 = ((f32[16,4,128]{2,1,0:T(4,128)}), f32[16,4,128]{2,1,0:T(4,128)S(1)}, u32[]{:S(2)}, u32[]{:S(2)}) async-start(f32[16,4,128]{2,1,0:T(4,128)} %get-tuple-element.13), calls=%async_computation.1 | async-start | bytes 65536 | tf_op jit(solution)/shard_map/all_to_all | solution.py:201
  26.6 11.9 %collective-permute-start.3 = (f32[32,128]{1,0:T(8,128)S(1)}, f32[32,128]{1,0:T(8,128)S(1)}, u32[]{:S(2)}, u32[]{:S(2)}) collective-permute-start(f32[32,128]{1,0:T(8,128)S(1)} %maximum_maximum_fusion.pack_ref.own_ref), channel_id=1, source_target_pairs={{0,496},{16,0},{32,16},{48,32},{64,48},{80,64},{96,80},{112,96},{1... | collective-permute-start | bytes 49160 | tf_op jit(solution)/shard_map/ppermute | solution.py:206
  40.4 23.8 %collective-permute-start.5 = (bf16[256,768]{1,0:T(8,128)(2,1)S(1)}, bf16[256,768]{1,0:T(8,128)(2,1)S(1)}, u32[]{:S(2)}, u32[]{:S(2)}) collective-permute-start(bf16[256,768]{1,0:T(8,128)(2,1)S(1)} %get-tuple-element.20), channel_id=1, source_target_pairs={{0,16},{16,32},{32,48},{48,64},{64,80},{80,96},{96,112},{112,128},... | collective-permute-start | bytes 1179656 | tf_op jit(solution)/shard_map/ppermute | solution.py:206
  42.4 55.5 %collective-permute-start = (bf16[256,768]{1,0:T(8,128)(2,1)S(1)}, bf16[256,768]{1,0:T(8,128)(2,1)S(1)}, u32[]{:S(2)}, u32[]{:S(2)}) collective-permute-start(bf16[256,768]{1,0:T(8,128)(2,1)S(1)} %get-tuple-element.12), channel_id=1, source_target_pairs={{0,32},{16,48},{32,64},{48,80},{64,96},{80,112},{96,128},{112,144}... | collective-permute-start | bytes 1179656 | tf_op jit(solution)/shard_map/ppermute | solution.py:206
  44.3 53.6 %collective-permute-start.2 = (bf16[256,768]{1,0:T(8,128)(2,1)S(1)}, bf16[256,768]{1,0:T(8,128)(2,1)S(1)}, u32[]{:S(2)}, u32[]{:S(2)}) collective-permute-start(bf16[256,768]{1,0:T(8,128)(2,1)S(1)} %collective-permute-done.1), channel_id=1, source_target_pairs={{8,32},{9,33},{10,34},{11,35},{12,36},{13,37},{14,38},{15,39},{24,... | collective-permute-start | bytes 1179656 | tf_op jit(solution)/shard_map/ppermute | solution.py:264
  64.3 39.3 %collective-permute-start.6 = (bf16[256,768]{1,0:T(8,128)(2,1)S(1)}, bf16[256,768]{1,0:T(8,128)(2,1)S(1)}, u32[]{:S(2)}, u32[]{:S(2)}) collective-permute-start(bf16[256,768]{1,0:T(8,128)(2,1)S(1)} %choose.1), channel_id=1, source_target_pairs={{0,496},{16,480},{32,464},{48,448},{64,432},{80,416},{96,400},{112... | collective-permute-start | bytes 1179656 | tf_op jit(solution)/shard_map/ppermute | solution.py:206
  88.2 9.7 %collective-permute-start.4 = (f32[80,128]{1,0:T(8,128)S(1)}, f32[80,128]{1,0:T(8,128)S(1)}, u32[]{:S(2)}, u32[]{:S(2)}) collective-permute-start(f32[80,128]{1,0:T(8,128)S(1)} %pack.1), channel_id=1, source_target_pairs={{0,32},{16,48},{32,64},{48,80},{64,96},{80,112},{96,128},{112,144}... | collective-permute-start | bytes 122888 | tf_op jit(solution)/shard_map/ppermute | solution.py:206
  92.2 11.4 %collective-permute-start.7 = (f32[80,128]{1,0:T(8,128)S(1)}, f32[80,128]{1,0:T(8,128)S(1)}, u32[]{:S(2)}, u32[]{:S(2)}) collective-permute-start(f32[80,128]{1,0:T(8,128)S(1)} %pack.1), channel_id=1, source_target_pairs={{0,480},{16,464},{32,448},{48,432},{64,416},{80,400},{96,384},{112... | collective-permute-start | bytes 122888 | tf_op jit(solution)/shard_map/ppermute | solution.py:206
where the time goes:
time: 107 us; the launch traced here: 106 us
  starting transfers between devices  55.2 us (52%)
  blocking collectives  28.3 us (26%)
  Pallas kernels  15.4 us (14%)
  waiting for transfers between devices  3.58 us (3%)
  between operations  2.12 us (2%)
  local copies, waits for them, and re-layouts  1.37 us (1%)
    ppermute x6, starting transfers between devices, send(): lax.ppermute(value, 'section', [(s, target(s) % count) for s in range(cou...  35.6 us
    all_to_all x2, blocking collectives, exchange(): return lax.all_to_all(parts, 'tensor', 0, 0, tiled=True)  28.3 us
    pallas_call x8, Pallas kernels, run(): pl.pallas_call(kernel, out_shape=out_shape, in_specs=[VMEM] * len(operand...  15.4 us
    all_to_all x2, starting transfers between devices, exchange(): return lax.all_to_all(parts, 'tensor', 0, 0, tiled=True)  14.2 us
    ppermute x1, starting transfers between devices, shards(): halfway = lax.ppermute(x[1], axes, around_x(0))  3.43 us
    all_to_all x2, waiting for transfers between devices, exchange(): return lax.all_to_all(parts, 'tensor', 0, 0, tiled=True)  2.14 us
  transfers between devices with their start and end apart: 10, of which 2 were waited for; matrix products, arithmetic and copies ran while one was open for 0% of the time, Pallas kernels for 11%

commit v1 on v0

--- a/solution.py
+++ b/solution.py
@@ -264,6 +264,7 @@
     moved1 = lax.ppermute(after(halfway, found), axes, around_x(1))
     ahead = send(after(own, found), lambda s: s - 1)
     parts.append(exchange(found))
+    y = after(y, moved0, moved1)
     y, pick, found = layer(1, "y", "pick", "sums")(y, parts[1], own, ahead)
     carry = send(after(pick, found), lambda s: s + 1)
     parts.append(exchange(found))

time: 107 us -> 102 us (0.953)
  the two profiles are of different devices: /device:TPU:8 before, /device:TPU:64 now
where the time goes in v1:
time: 102 us; the launch traced here: 101 us
  starting transfers between devices  44 us (43%)
  blocking collectives  24.8 us (24%)
  Pallas kernels  15.4 us (15%)
  waiting for transfers between devices  12.6 us (12%)
  local copies, waits for them, and re-layouts  2.11 us (2%)
  between operations  2.08 us (2%)
    all_to_all x2, blocking collectives, exchange(): return lax.all_to_all(parts, 'tensor', 0, 0, tiled=True)  24.8 us
    ppermute x6, starting transfers between devices, send(): lax.ppermute(value, 'section', [(s, target(s) % count) for s in range(cou...  23 us
    pallas_call x8, Pallas kernels, run(): pl.pallas_call(kernel, out_shape=out_shape, in_specs=[VMEM] * len(operand...  15.4 us
    all_to_all x2, starting transfers between devices, exchange(): return lax.all_to_all(parts, 'tensor', 0, 0, tiled=True)  13.3 us
    all_to_all x2, waiting for transfers between devices, exchange(): return lax.all_to_all(parts, 'tensor', 0, 0, tiled=True)  7.45 us
    ppermute x1, starting transfers between devices, shards(): moved1 = lax.ppermute(after(halfway, found), axes, around_x(1))  4.3 us
    ppermute x6, waiting for transfers between devices, send(): lax.ppermute(value, 'section', [(s, target(s) % count) for s in range(cou...  3.48 us
    ppermute x1, starting transfers between devices, shards(): halfway = lax.ppermute(x[1], axes, around_x(0))  3.4 us
  transfers between devices with their start and end apart: 10, of which 5 were waited for; matrix products, arithmetic and copies ran while one was open for 0% of the time, Pallas kernels for 11%

profile of v1, /device:TPU:64, one launch (start us, length us, event | category | flops | bytes accessed | tf_op | source)
XLA Modules:
  0.0 101.2 jit_solution(7973437052158433746)
XLA Ops:
  0.6 0.0 copy-start
  0.6 1.2 %slice_bitcast_fusion = (bf16[256,768]{1,0:T(8,128)(2,1)S(1)}, bf16[256,768]{1,0:T(8,128)(2,1)S(1)}) fusion(bf16[1,2,256,768]{3,2,1,0:T(8,128)(2,1)} %param.5), kind=kLoop, calls=%fused_computation | loop fusion | bytes 1572864 | tf_op jit(solution)/shard_map/squeeze | solution.py:259
  1.9 3.4 %collective-permute-start.1 = (bf16[256,768]{1,0:T(8,128)(2,1)S(1)}, bf16[256,768]{1,0:T(8,128)(2,1)S(1)}, u32[]{:S(2)}, u32[]{:S(2)}) collective-permute-start(bf16[256,768]{1,0:T(8,128)(2,1)S(1)} %get-tuple-element.24), channel_id=1, source_target_pairs={{0,8},{1,9},{2,10},{3,11},{4,12},{5,13},{6,14},{7,15},{16,24},{17,... | collective-permute-start | bytes 1179656 | tf_op jit(solution)/shard_map/ppermute | solution.py:259
  5.3 0.0 copy-done
  5.3 0.8 first_sums.1
  6.1 8.1 %all-to-all-start = ((f32[16,4,128]{2,1,0:T(4,128)}), f32[16,4,128]{2,1,0:T(4,128)S(1)}, u32[]{:S(2)}, u32[]{:S(2)}) async-start(f32[16,4,128]{2,1,0:T(4,128)} %first_sums.1), calls=%async_computation | async-start | bytes 65536 | tf_op jit(solution)/shard_map/all_to_all | solution.py:201
  14.3 0.0 copy-start.1
  14.3 3.7 %collective-permute-start = (bf16[256,768]{1,0:T(8,128)(2,1)S(1)}, bf16[256,768]{1,0:T(8,128)(2,1)S(1)}, u32[]{:S(2)}, u32[]{:S(2)}) collective-permute-start(bf16[256,768]{1,0:T(8,128)(2,1)S(1)} %get-tuple-element.13), channel_id=1, source_target_pairs={{0,32},{16,48},{32,64},{48,80},{64,96},{80,112},{96,128},{112,144}... | collective-permute-start | bytes 1179656 | tf_op jit(solution)/shard_map/ppermute | solution.py:206
  19.3 0.1 add_convert_fusion
  19.4 0.1 pad.2.clone
  19.5 0.1 pad.3.clone
  19.5 0.0 copy-done.1
  19.5 0.0 copy-start.2
  19.6 0.7 copy-done.2
  20.2 0.1 maximum_maximum_fusion.pack_ref.own_ref
  20.3 2.6 %all-to-all-done.parts_ref.refs_0_ = f32[16,4,128]{2,1,0:T(4,128)S(1)} async-done(((f32[16,4,128]{2,1,0:T(4,128)}), f32[16,4,128]{2,1,0:T(4,128)S(1)}, u32[]{:S(2)}, u32[]{:S(2)}) %all-to-all-start) | async-done | bytes 32800 | tf_op jit(solution)/shard_map/all_to_all | solution.py:201
  22.9 2.4 %layer.3 = (bf16[2,256,768]{2,1,0:T(8,128)(2,1)S(1)}, f32[16,4,128]{2,1,0:T(4,128)}) custom-call(bf16[2,256,768]{2,1,0:T(8,128)(2,1)S(1)} %bitcast.8, f32[16,4,128]{2,1,0:T(4,128)S(1)} %all-to-all-done.parts_ref.refs_0_, f32[32,128]{1,0:T(8,128)S(1)} %maximum_maximum_fusion.pack_ref.own_ref), custom_call_target="tpu_custom_call" | custom-call | flops 400000000 | bytes 1000000 | tf_op jit(solution)/shard_map/layer/pallas_call | solution.py:26
  25.3 0.0 collective-permute-done.1
  25.3 4.3 %collective-permute-start.2 = (bf16[256,768]{1,0:T(8,128)(2,1)S(1)}, bf16[256,768]{1,0:T(8,128)(2,1)S(1)}, u32[]{:S(2)}, u32[]{:S(2)}) collective-permute-start(bf16[256,768]{1,0:T(8,128)(2,1)S(1)} %collective-permute-done.1), channel_id=1, source_target_pairs={{8,32},{9,33},{10,34},{11,35},{12,36},{13,37},{14,38},{15,39},{24,... | collective-permute-start | bytes 1179656 | tf_op jit(solution)/shard_map/ppermute | solution.py:264
  29.6 5.2 %all-to-all-start.1 = ((f32[16,4,128]{2,1,0:T(4,128)}), f32[16,4,128]{2,1,0:T(4,128)S(1)}, u32[]{:S(2)}, u32[]{:S(2)}) async-start(f32[16,4,128]{2,1,0:T(4,128)} %get-tuple-element.14), calls=%async_computation.1 | async-start | bytes 65536 | tf_op jit(solution)/shard_map/all_to_all | solution.py:201
  34.8 1.9 %collective-permute-start.3 = (f32[32,128]{1,0:T(8,128)S(1)}, f32[32,128]{1,0:T(8,128)S(1)}, u32[]{:S(2)}, u32[]{:S(2)}) collective-permute-start(f32[32,128]{1,0:T(8,128)S(1)} %maximum_maximum_fusion.pack_ref.own_ref), channel_id=1, source_target_pairs={{0,496},{16,0},{32,16},{48,32},{64,48},{80,64},{96,80},{112,96},{1... | collective-permute-start | bytes 49160 | tf_op jit(solution)/shard_map/ppermute | solution.py:206
  36.7 0.0 collective-permute-done.x0_ref
  36.7 1.7 %collective-permute-done.2.x1_ref = bf16[256,768]{1,0:T(8,128)(2,1)S(1)} collective-permute-done((bf16[256,768]{1,0:T(8,128)(2,1)S(1)}, bf16[256,768]{1,0:T(8,128)(2,1)S(1)}, u32[]{:S(2)}, u32[]{:S(2)}) %collective-permute-start.2) | collective-permute-done | bytes 393248 | tf_op jit(solution)/shard_map/ppermute | solution.py:264
  38.4 0.0 collective-permute-done.3.refs_0_.pack_ref.next_ref
  38.4 4.9 %all-to-all-done.1.parts_ref.refs_1_ = f32[16,4,128]{2,1,0:T(4,128)S(1)} async-done(((f32[16,4,128]{2,1,0:T(4,128)}), f32[16,4,128]{2,1,0:T(4,128)S(1)}, u32[]{:S(2)}, u32[]{:S(2)}) %all-to-all-start.1) | async-done | bytes 32800 | tf_op jit(solution)/shard_map/all_to_all | solution.py:201
  43.3 2.0 %layer.4 = (bf16[2,256,768]{2,1,0:T(8,128)(2,1)S(1)}, bf16[256,768]{1,0:T(8,128)(2,1)S(1)}, f32[16,4,128]{2,1,0:T(4,128)S(1)}) custom-call(bf16[2,256,768]{2,1,0:T(8,128)(2,1)S(1)} %get-tuple-element.18.x_ref, f32[16,4,128]{2,1,0:T(4,128)S(1)} %all-to-all-done.1.parts_ref.refs_1_, f32[32,128]{1,0:T(8,128)S(1)} %maximum_maximum_fusion.pack_ref.own_ref, ...), custom_call_target="tpu_custom_call" | custom-call | flops 400000000 | bytes 1000000 | tf_op jit(solution)/shard_map/layer/pallas_call | solution.py:26
  45.3 1.9 %collective-permute-start.5 = (bf16[256,768]{1,0:T(8,128)(2,1)S(1)}, bf16[256,768]{1,0:T(8,128)(2,1)S(1)}, u32[]{:S(2)}, u32[]{:S(2)}) collective-permute-start(bf16[256,768]{1,0:T(8,128)(2,1)S(1)} %get-tuple-element.22), channel_id=1, source_target_pairs={{0,16},{16,32},{32,48},{48,64},{64,80},{80,96},{96,112},{112,128},... | collective-permute-start | bytes 1179656 | tf_op jit(solution)/shard_map/ppermute | solution.py:206
  47.2 13.7 %all_to_all.20.parts_ref.refs_2_ = f32[16,4,128]{2,1,0:T(4,128)S(1)} all-to-all(f32[16,4,128]{2,1,0:T(4,128)S(1)} %get-tuple-element.19), channel_id=1, replica_groups=mesh['section'=32,'tensor'=16] {'tensor'}, dimensions={0} | all-to-all | bytes 65536 | tf_op jit(solution)/shard_map/all_to_all | solution.py:201
  61.0 1.8 %layer.5 = f32[16,4,128]{2,1,0:T(4,128)S(1)} custom-call(bf16[2,256,768]{2,1,0:T(8,128)(2,1)S(1)} %get-tuple-element.20.x_ref.y_ref, f32[16,4,128]{2,1,0:T(4,128)S(1)} %all_to_all.20.parts_ref.refs_2_, f32[32,128]{1,0:T(8,128)S(1)} %collective-permute-done.3.refs_0_.pack_ref.next_ref), custom_call_target="tpu_custom_call" | custom-call | flops 400000000 | bytes 1000000 | tf_op jit(solution)/shard_map/layer/pallas_call | solution.py:26
  62.8 0.0 collective-permute-done.5.carry_ref
  62.8 0.2 choose.1
  62.9 9.3 %collective-permute-start.6 = (bf16[256,768]{1,0:T(8,128)(2,1)S(1)}, bf16[256,768]{1,0:T(8,128)(2,1)S(1)}, u32[]{:S(2)}, u32[]{:S(2)}) collective-permute-start(bf16[256,768]{1,0:T(8,128)(2,1)S(1)} %choose.1), channel_id=1, source_target_pairs={{0,496},{16,480},{32,464},{48,448},{64,432},{80,416},{96,400},{112... | collective-permute-start | bytes 1179656 | tf_op jit(solution)/shard_map/ppermute | solution.py:206
  72.2 11.1 %all_to_all.21.refs_3_ = f32[16,4,128]{2,1,0:T(4,128)S(1)} all-to-all(f32[16,4,128]{2,1,0:T(4,128)S(1)} %layer.5), channel_id=1, replica_groups=mesh['section'=32,'tensor'=16] {'tensor'}, dimensions={0} | all-to-all | bytes 65536 | tf_op jit(solution)/shard_map/all_to_all | solution.py:201
  83.3 4.1 %collective-permute-start.4 = (f32[80,128]{1,0:T(8,128)S(1)}, f32[80,128]{1,0:T(8,128)S(1)}, u32[]{:S(2)}, u32[]{:S(2)}) collective-permute-start(f32[80,128]{1,0:T(8,128)S(1)} %pack.1), channel_id=1, source_target_pairs={{0,32},{16,48},{32,64},{48,80},{64,96},{80,112},{96,128},{112,144}... | collective-permute-start | bytes 122888 | tf_op jit(solution)/shard_map/ppermute | solution.py:206
  87.4 2.1 %collective-permute-start.7 = (f32[80,128]{1,0:T(8,128)S(1)}, f32[80,128]{1,0:T(8,128)S(1)}, u32[]{:S(2)}, u32[]{:S(2)}) collective-permute-start(f32[80,128]{1,0:T(8,128)S(1)} %pack.1), channel_id=1, source_target_pairs={{0,480},{16,464},{32,448},{48,432},{64,416},{80,400},{96,384},{112... | collective-permute-start | bytes 122888 | tf_op jit(solution)/shard_map/ppermute | solution.py:206
  89.5 2.3 %collective-permute-done.4.pack_ref = f32[80,128]{1,0:T(8,128)S(1)} collective-permute-done((f32[80,128]{1,0:T(8,128)S(1)}, f32[80,128]{1,0:T(8,128)S(1)}, u32[]{:S(2)}, u32[]{:S(2)}) %collective-permute-start.4) | collective-permute-done | bytes 40992 | tf_op jit(solution)/shard_map/ppermute | solution.py:206
  91.9 5.7 %repeat.1 = bf16[2,256,768]{2,1,0:T(8,128)(2,1)} custom-call(bf16[256,768]{1,0:T(8,128)(2,1)S(1)} %collective-permute-done.x0_ref, bf16[256,768]{1,0:T(8,128)(2,1)S(1)} %collective-permute-done.2.x1_ref, f32[80,128]{1,0:T(8,128)S(1)} %collective-permute-done.4.pack_ref), custom_call_target="tpu_custom_call" | custom-call | flops 1600000000 | bytes 1000000 | tf_op jit(solution)/shard_map/repeat/pallas_call | solution.py:26
  97.6 1.1 %collective-permute-done.7.pack_ref = f32[80,128]{1,0:T(8,128)S(1)} collective-permute-done((f32[80,128]{1,0:T(8,128)S(1)}, f32[80,128]{1,0:T(8,128)S(1)}, u32[]{:S(2)}, u32[]{:S(2)}) %collective-permute-start.7) | collective-permute-done | bytes 40992 | tf_op jit(solution)/shard_map/ppermute | solution.py:206
  98.7 0.0 collective-permute-done.6.x_ref
  98.7 2.4 %mirror.1 = bf16[256,768]{1,0:T(8,128)(2,1)} custom-call(bf16[256,768]{1,0:T(8,128)(2,1)S(1)} %collective-permute-done.6.x_ref, f32[80,128]{1,0:T(8,128)S(1)} %collective-permute-done.7.pack_ref), custom_call_target="tpu_custom_call" | custom-call | flops 400000000 | bytes 1000000 | tf_op jit(solution)/shard_map/mirror/pallas_call | solution.py:26
  (4 shorter events, 0.1 us)
Async XLA Ops:
  0.6 4.7 %copy-start = (bf16[1,2,256,768]{3,2,1,0:T(8,128)(2,1)S(1)}, bf16[1,2,256,768]{3,2,1,0:T(8,128)(2,1)}, u32[]{:S(2)}) copy-start(bf16[1,2,256,768]{3,2,1,0:T(8,128)(2,1)} %param.5) | copy-start | bytes 2359300
  1.9 23.4 %collective-permute-start.1 = (bf16[256,768]{1,0:T(8,128)(2,1)S(1)}, bf16[256,768]{1,0:T(8,128)(2,1)S(1)}, u32[]{:S(2)}, u32[]{:S(2)}) collective-permute-start(bf16[256,768]{1,0:T(8,128)(2,1)S(1)} %get-tuple-element.24), channel_id=1, source_target_pairs={{0,8},{1,9},{2,10},{3,11},{4,12},{5,13},{6,14},{7,15},{16,24},{17,... | collective-permute-start | bytes 1179656 | tf_op jit(solution)/shard_map/ppermute | solution.py:259
  6.1 16.7 %all-to-all-start = ((f32[16,4,128]{2,1,0:T(4,128)}), f32[16,4,128]{2,1,0:T(4,128)S(1)}, u32[]{:S(2)}, u32[]{:S(2)}) async-start(f32[16,4,128]{2,1,0:T(4,128)} %first_sums.1), calls=%async_computation | async-start | bytes 65536 | tf_op jit(solution)/shard_map/all_to_all | solution.py:201
  14.3 5.3 %copy-start.1 = (f32[1,2,768]{2,1,0:T(2,128)S(1)}, f32[1,2,768]{2,1,0:T(2,128)}, u32[]{:S(2)}) copy-start(f32[1,2,768]{2,1,0:T(2,128)} %param.6) | copy-start | bytes 18436
  14.3 22.4 %collective-permute-start = (bf16[256,768]{1,0:T(8,128)(2,1)S(1)}, bf16[256,768]{1,0:T(8,128)(2,1)S(1)}, u32[]{:S(2)}, u32[]{:S(2)}) collective-permute-start(bf16[256,768]{1,0:T(8,128)(2,1)S(1)} %get-tuple-element.13), channel_id=1, source_target_pairs={{0,32},{16,48},{32,64},{48,80},{64,96},{80,112},{96,128},{112,144}... | collective-permute-start | bytes 1179656 | tf_op jit(solution)/shard_map/ppermute | solution.py:206
  19.5 0.7 copy-start.2
  25.3 13.1 %collective-permute-start.2 = (bf16[256,768]{1,0:T(8,128)(2,1)S(1)}, bf16[256,768]{1,0:T(8,128)(2,1)S(1)}, u32[]{:S(2)}, u32[]{:S(2)}) collective-permute-start(bf16[256,768]{1,0:T(8,128)(2,1)S(1)} %collective-permute-done.1), channel_id=1, source_target_pairs={{8,32},{9,33},{10,34},{11,35},{12,36},{13,37},{14,38},{15,39},{24,... | collective-permute-start | bytes 1179656 | tf_op jit(solution)/shard_map/ppermute | solution.py:264
  29.6 13.7 %all-to-all-start.1 = ((f32[16,4,128]{2,1,0:T(4,128)}), f32[16,4,128]{2,1,0:T(4,128)S(1)}, u32[]{:S(2)}, u32[]{:S(2)}) async-start(f32[16,4,128]{2,1,0:T(4,128)} %get-tuple-element.14), calls=%async_computation.1 | async-start | bytes 65536 | tf_op jit(solution)/shard_map/all_to_all | solution.py:201
  34.8 3.6 %collective-permute-start.3 = (f32[32,128]{1,0:T(8,128)S(1)}, f32[32,128]{1,0:T(8,128)S(1)}, u32[]{:S(2)}, u32[]{:S(2)}) collective-permute-start(f32[32,128]{1,0:T(8,128)S(1)} %maximum_maximum_fusion.pack_ref.own_ref), channel_id=1, source_target_pairs={{0,496},{16,0},{32,16},{48,32},{64,48},{80,64},{96,80},{112,96},{1... | collective-permute-start | bytes 49160 | tf_op jit(solution)/shard_map/ppermute | solution.py:206
  45.3 17.5 %collective-permute-start.5 = (bf16[256,768]{1,0:T(8,128)(2,1)S(1)}, bf16[256,768]{1,0:T(8,128)(2,1)S(1)}, u32[]{:S(2)}, u32[]{:S(2)}) collective-permute-start(bf16[256,768]{1,0:T(8,128)(2,1)S(1)} %get-tuple-element.22), channel_id=1, source_target_pairs={{0,16},{16,32},{32,48},{48,64},{64,80},{80,96},{96,112},{112,128},... | collective-permute-start | bytes 1179656 | tf_op jit(solution)/shard_map/ppermute | solution.py:206
  62.9 35.8 %collective-permute-start.6 = (bf16[256,768]{1,0:T(8,128)(2,1)S(1)}, bf16[256,768]{1,0:T(8,128)(2,1)S(1)}, u32[]{:S(2)}, u32[]{:S(2)}) collective-permute-start(bf16[256,768]{1,0:T(8,128)(2,1)S(1)} %choose.1), channel_id=1, source_target_pairs={{0,496},{16,480},{32,464},{48,448},{64,432},{80,416},{96,400},{112... | collective-permute-start | bytes 1179656 | tf_op jit(solution)/shard_map/ppermute | solution.py:206
  83.3 8.5 %collective-permute-start.4 = (f32[80,128]{1,0:T(8,128)S(1)}, f32[80,128]{1,0:T(8,128)S(1)}, u32[]{:S(2)}, u32[]{:S(2)}) collective-permute-start(f32[80,128]{1,0:T(8,128)S(1)} %pack.1), channel_id=1, source_target_pairs={{0,32},{16,48},{32,64},{48,80},{64,96},{80,112},{96,128},{112,144}... | collective-permute-start | bytes 122888 | tf_op jit(solution)/shard_map/ppermute | solution.py:206
  87.4 11.3 %collective-permute-start.7 = (f32[80,128]{1,0:T(8,128)S(1)}, f32[80,128]{1,0:T(8,128)S(1)}, u32[]{:S(2)}, u32[]{:S(2)}) collective-permute-start(f32[80,128]{1,0:T(8,128)S(1)} %pack.1), channel_id=1, source_target_pairs={{0,480},{16,464},{32,448},{48,432},{64,416},{80,400},{96,384},{112... | collective-permute-start | bytes 122888 | tf_op jit(solution)/shard_map/ppermute | solution.py:206
